TPU v7x, 256 devices: a whole 4x4x8 slice. The times are simulated.
256 devices in a mesh: dp: 32 (over y, x, core), expert: 8 (over z).
Axes of the slice: x: 4, y: 4, z: 8, core: 2. Of those that a mesh axis runs over, the one named last changes fastest.
Arguments:
- gradients: bfloat16 [8, 8, 3584, 1024], P('expert', None, 'dp')
- owners: int32 [8, 8], P('expert'), may hold values from 0 to 7, as said below
Outputs:
- update: bfloat16 [8, 8, 3584, 1024], P('expert', None, 'dp')
- rms_table: float32 [8, 8], replicated
- owned_rms: float32 [8, 32], P('expert', 'dp')
Inputs may be any that keep to these rules, and one draw needn't show every extreme that they name: Entry [g, j] is the team that orthogonalizes matrix j of group g; team t is the devices 4 t to 4 t + 3 along dp. Each row owners[g] is a permutation of the 8 teams.
All inputs are finite; a program needn't handle non-finite values.
Results may differ from a plain program's by a relative error of at most 0.0067.
Values may be sent and summed in bfloat16 or wider, within the bound.
A program may use at most 64 MiB of HBM per device.

v0:
```python
import functools
import math

import jax
import jax.numpy as jnp
from jax import lax
from jax.experimental import pallas as pl
from jax.experimental.pallas import tpu as pltpu
from jax.sharding import PartitionSpec as P

COEF_A = 3.4445
COEF_B = -4.775
COEF_C = 2.0315

RING = 4
BLK = 256
HALF = BLK // 2
EARLY = 3 * BLK
PIECE = BLK + HALF

F32 = jnp.float32
BF16 = jnp.bfloat16


def dot(a, b):
    return lax.dot_general(a, b, (((1,), (0,)), ((), ())), preferred_element_type=F32)


def dot_t(a, b):
    return lax.dot_general(a, b, (((0,), (0,)), ((), ())), preferred_element_type=F32)


def kernel(
    total_rows,
    n_groups,
    g_ref,
    u_ref,
    whole_ref,
    x_ref,
    pa_ref,
    pb_ref,
    ra_ref,
    rb_ref,
    aa_ref,
    ab_ref,
    tr_ref,
    s_ref,
    e1_ref,
    r_ref,
    a1_ref,
    e2_ref,
    e_ref,
    y_ref,
    rms_ref,
    tab_ref,
    local_sem,
    in_send,
    in_recv,
    rs_send,
    rs_recv,
    ag_send,
    ag_recv,
    tr_send,
    tr_recv,
    out_send,
    out_recv,
    rms_send,
    rms_recv,
    tab_send,
    tab_recv,
):
    rows = g_ref.shape[2]
    cols = g_ref.shape[3]
    d = lax.axis_index("dp")
    group = lax.axis_index("expert")
    c = lax.rem(d, 2)
    x = lax.rem(d // 2, RING)
    y = d // (2 * RING)
    p = jnp.where(c == 0, x, y)
    q = jnp.where(c == 0, y, x)
    p_stride = jnp.where(c == 0, 2, 2 * RING)
    q_stride = jnp.where(c == 0, 2 * RING, 2)
    chip = d - c
    mine = c * RING + p

    def along_p(offset, core):
        return chip + (lax.rem(p + offset, RING) - p) * p_stride + core

    def along_q(offset, core):
        return chip + (lax.rem(q + offset, RING) - q) * q_stride + core

    def remote(src, dst, send, recv, dp, to_group=group):
        return pltpu.make_async_remote_copy(
            src_ref=src,
            dst_ref=dst,
            send_sem=send,
            recv_sem=recv,
            device_id=(dp, to_group),
            device_id_type=pl.DeviceIdType.MESH,
        )

    barrier = pltpu.get_barrier_semaphore()
    greeted = []
    for offset in range(RING):
        for core in (c, 1 - c):
            if offset == 0 and core is c:
                continue
            greeted.append((along_p(offset, core), group))
    for offset in range(1, RING):
        for core in (c, 1 - c):
            greeted.append((along_q(offset, core), group))
    for offset in range(1, n_groups):
        greeted.append((d, lax.rem(group + offset, n_groups)))
    for who in greeted:
        pl.semaphore_signal(barrier, inc=1, device_id=who, device_id_type=pl.DeviceIdType.MESH)
    own = pltpu.make_async_copy(
        g_ref.at[0, mine], x_ref.at[pl.ds(pl.multiple_of(c * rows, 16), rows)], local_sem.at[0]
    )
    own.start()
    pl.semaphore_wait(barrier, len(greeted))

    parts = (pl.ds(0, EARLY), pl.ds(EARLY, cols - EARLY))

    def slot(offset, core, part):
        return x_ref.at[pl.ds(pl.multiple_of((2 * offset + core) * rows, 16), rows), part]

    sent = []
    for number, part in enumerate(parts):
        for offset in (2, 1, 3, 0):
            back = (RING - offset) % RING
            if offset:
                copy = remote(
                    g_ref.at[0, c * RING + lax.rem(p + back, RING), :, part],
                    slot(offset, c, part),
                    in_send.at[number, 2 * offset],
                    in_recv.at[number, 2 * offset + c],
                    along_p(back, c),
                )
                copy.start()
                sent.append(copy)
            copy = remote(
                g_ref.at[0, (1 - c) * RING + lax.rem(q + back, RING), :, part],
                slot(offset, c, part),
                in_send.at[number, 2 * offset + 1],
                in_recv.at[number, 2 * offset + c],
                along_q(back, 1 - c),
            )
            copy.start()
            sent.append(copy)

    def arrive(number):
        part = parts[number]
        for offset, core in ((0, 1 - c), (1, 0), (1, 1), (3, 0), (3, 1), (2, 0), (2, 1)):
            remote(
                g_ref.at[0, 0, :, part],
                slot(offset, core, part),
                in_send.at[number, 0],
                in_recv.at[number, 2 * offset + core],
                d,
            ).wait_recv()

    diag = lax.broadcasted_iota(jnp.int32, (BLK, BLK), 0) == lax.broadcasted_iota(
        jnp.int32, (BLK, BLK), 1
    )

    def on_diag(value):
        return jnp.sum(jnp.where(diag, value, 0.0), axis=0, keepdims=True)

    own.wait()
    arrive(0)
    value = dot_t(x_ref[:, pl.ds(0, BLK)], x_ref[:, pl.ds(0, BLK)])
    total = on_diag(value)
    pa_ref[0, pl.ds(0, BLK)] = value.astype(BF16)
    value = dot_t(x_ref[:, pl.ds(BLK, BLK)], x_ref[:, pl.ds(0, 2 * BLK)])
    total += on_diag(value[:, BLK:])
    pa_ref[0, pl.ds(BLK, HALF)] = value[:HALF, :BLK].astype(BF16)
    pa_ref[1, pl.ds(BLK, HALF)] = value[HALF:, :BLK].astype(BF16)
    pa_ref[1, pl.ds(0, BLK)] = value[:, BLK:].astype(BF16)
    value = dot_t(x_ref[:, pl.ds(2 * BLK, BLK)], x_ref[:, pl.ds(0, 3 * BLK)])
    total += on_diag(value[:, 2 * BLK :])
    pa_ref[2, pl.ds(BLK, HALF)] = value[:HALF, :BLK].astype(BF16)
    pa_ref[3, pl.ds(BLK, HALF)] = value[HALF:, :BLK].astype(BF16)
    pa_ref[3, pl.ds(0, BLK)] = value[:, BLK : 2 * BLK].astype(BF16)
    pa_ref[2, pl.ds(0, BLK)] = value[:, 2 * BLK :].astype(BF16)

    def scatter(number, piece_ref, got_ref):
        for offset in (2, 1, 3):
            copy = remote(
                piece_ref.at[lax.rem(q + offset, RING)],
                got_ref.at[RING - 1 - offset],
                rs_send.at[number, offset - 1],
                rs_recv.at[number, RING - 1 - offset],
                along_q(offset, c),
            )
            copy.start()
            sent.append(copy)

    def add_up(number, piece_ref, got_ref, all_ref):
        for index in range(RING - 1):
            remote(
                piece_ref.at[0], got_ref.at[index], rs_send.at[number, 0], rs_recv.at[number, index], d
            ).wait_recv()
        all_ref[q] = (
            (piece_ref[q].astype(F32) + got_ref[0].astype(F32))
            + (got_ref[1].astype(F32) + got_ref[2].astype(F32))
        ).astype(BF16)
        for offset in (2, 1, 3):
            copy = remote(
                all_ref.at[q],
                all_ref.at[q],
                ag_send.at[number, offset - 1],
                ag_recv.at[number, q],
                along_q(offset, c),
            )
            copy.start()
            sent.append(copy)

    def collect(number, all_ref):
        for offset in (1, 3, 2):
            k = lax.rem(q + offset, RING)
            remote(
                all_ref.at[k], all_ref.at[k], ag_send.at[number, 0], ag_recv.at[number, k], d
            ).wait_recv()

    scatter(0, pa_ref, ra_ref)

    arrive(1)
    value = dot_t(x_ref[:, pl.ds(EARLY, BLK)], x_ref[...])
    total += on_diag(value[:, EARLY:])
    for k in range(RING):
        pb_ref[k] = value[:, k * BLK : (k + 1) * BLK].astype(BF16)
    scatter(1, pb_ref, rb_ref)
    tr_ref[q] = jnp.broadcast_to(jnp.sum(total, axis=1, keepdims=True), (8, 128))
    for offset in (2, 1, 3):
        copy = remote(
            tr_ref.at[q], tr_ref.at[q], tr_send.at[offset - 1], tr_recv.at[q], along_q(offset, c)
        )
        copy.start()
        sent.append(copy)
    add_up(0, pa_ref, ra_ref, aa_ref)
    add_up(1, pb_ref, rb_ref, ab_ref)

    for offset in (1, 3, 2):
        k = lax.rem(q + offset, RING)
        remote(tr_ref.at[k], tr_ref.at[k], tr_send.at[0], tr_recv.at[k], d).wait_recv()
    trace = ((tr_ref[0] + tr_ref[1]) + (tr_ref[2] + tr_ref[3]))[0:1, 0:1]
    scale = 1.0 / jnp.sqrt(trace + 1e-06)
    rms = jnp.sqrt(trace / (total_rows * cols))
    rms_ref[mine] = jnp.broadcast_to(rms, (8, 128))
    number = 0
    for offset in range(RING):
        for core in (c, 1 - c):
            if offset == 0 and core is c:
                continue
            copy = remote(
                rms_ref.at[mine],
                rms_ref.at[mine],
                rms_send.at[number],
                rms_recv.at[mine],
                along_p(offset, core),
            )
            copy.start()
            sent.append(copy)
            number += 1

    square = scale * scale

    def block(i):
        return pl.ds(i * BLK, BLK)

    collect(0, aa_ref)
    for k, (i, j) in enumerate(((0, 0), (1, 1), (2, 2), (2, 1))):
        one = (aa_ref[k, pl.ds(0, BLK)].astype(F32) * square).astype(BF16)
        s_ref[block(i), block(j)] = one
        if i != j:
            s_ref[block(j), block(i)] = one.T
        high = pl.ds((1 + k // 2) * BLK + (k % 2) * HALF, HALF)
        one = (aa_ref[k, pl.ds(BLK, HALF)].astype(F32) * square).astype(BF16)
        s_ref[high, block(0)] = one
        s_ref[block(0), high] = one.T
    collect(1, ab_ref)
    for k in range(RING):
        one = (ab_ref[k].astype(F32) * square).astype(BF16)
        s_ref[block(3), block(k)] = one
        if k < 3:
            s_ref[block(k), block(3)] = one.T

    def product(out_ref, left, right, plus, by, times):
        for i in range(RING):
            wide = pl.ds(0, (i + 1) * BLK)
            value = by * plus[block(i), wide].astype(F32) + times * dot(
                left[block(i), :], right[:, wide]
            )
            value = value.astype(BF16)
            out_ref[block(i), wide] = value
            for j in range(i):
                out_ref[block(j), block(i)] = value[:, j * BLK : (j + 1) * BLK].T

    product(e1_ref, s_ref, s_ref, s_ref, COEF_B, COEF_C)

    for offset in range(1, RING):
        other = c * RING + lax.rem(p + offset, RING)
        remote(rms_ref.at[other], rms_ref.at[other], rms_send.at[0], rms_recv.at[other], d).wait_recv()
    for index in range(RING):
        other = (1 - c) * RING + index
        remote(rms_ref.at[other], rms_ref.at[other], rms_send.at[0], rms_recv.at[other], d).wait_recv()
    lane = lax.broadcasted_iota(jnp.int32, (8, 128), 1)
    line = jnp.zeros((8, 128), F32)
    for index in range(2 * RING):
        line = jnp.where(lane == index, rms_ref[index], line)
    tab_ref[group] = line
    for offset in range(1, n_groups):
        copy = remote(
            tab_ref.at[group],
            tab_ref.at[group],
            tab_send.at[offset - 1],
            tab_recv.at[group],
            d,
            lax.rem(group + offset, n_groups),
        )
        copy.start()
        sent.append(copy)

    product(r_ref, e1_ref, s_ref, s_ref, COEF_A, 1.0)
    product(a1_ref, e1_ref, r_ref, r_ref, COEF_A, 1.0)
    product(e2_ref, a1_ref, a1_ref, a1_ref, COEF_B, COEF_C)

    factor = math.sqrt(total_rows) * scale
    for n in range(RING):
        both = e1_ref[:, block(n)].astype(F32) + e2_ref[:, block(n)].astype(F32)
        e_ref[:, block(n)] = (COEF_A * both + dot(e1_ref[...], e2_ref[:, block(n)])).astype(BF16)
        value = COEF_A * COEF_A * x_ref[:, block(n)].astype(F32) + dot(
            x_ref[...], e_ref[:, block(n)]
        )
        y_ref[:, block(n)] = (factor * value).astype(BF16)

        def home(offset, core):
            return y_ref.at[
                pl.ds(pl.multiple_of((2 * offset + core) * rows, 16), rows), block(n)
            ]

        for offset, core in ((2, 0), (2, 1), (1, 0), (1, 1), (3, 0), (3, 1), (0, 1 - c)):
            remote(
                home(offset, core),
                u_ref.at[mine, :, block(n)],
                out_send.at[2 * offset + core],
                out_recv.at[mine],
                along_p(offset, core),
            ).start()
        pltpu.make_async_copy(home(0, c), u_ref.at[mine, :, block(n)], local_sem.at[1]).start()

    for offset in range(1, n_groups):
        other = lax.rem(group + offset, n_groups)
        remote(
            tab_ref.at[other], tab_ref.at[other], tab_send.at[0], tab_recv.at[other], d
        ).wait_recv()
    sub = lax.broadcasted_iota(jnp.int32, (8, 128), 0)
    whole = jnp.zeros((8, 128), F32)
    for index in range(n_groups):
        whole = jnp.where(sub == index, tab_ref[index], whole)
    whole_ref[...] = whole

    def all_columns(other, offset, core):
        return remote(
            y_ref.at[pl.ds(pl.multiple_of((2 * offset + core) * rows, 16), rows)],
            u_ref.at[other],
            out_send.at[2 * offset + core],
            out_recv.at[other],
            d,
        )

    pltpu.make_async_copy(y_ref.at[pl.ds(0, rows)], u_ref.at[mine], local_sem.at[1]).wait()
    for offset in range(1, RING):
        all_columns(c * RING + lax.rem(p + offset, RING), 0, 0).wait_recv()
    for index in range(RING):
        all_columns((1 - c) * RING + index, 0, 0).wait_recv()
    for offset, core in ((2, 0), (2, 1), (1, 0), (1, 1), (3, 0), (3, 1), (0, 1 - c)):
        all_columns(mine, offset, core).wait_send()
    for copy in sent:
        copy.wait_send()


def finish(n_groups, u_ref, whole_ref, owners_ref, update_ref, table_ref, owned_ref, sem):
    mats = u_ref.shape[0]
    copies = [
        pltpu.make_async_copy(u_ref.at[m], update_ref.at[0, m], sem.at[m]) for m in range(mats)
    ]
    for copy in copies:
        copy.start()
    table = whole_ref[...][0:n_groups, 0:mats]
    table_ref[...] = table
    sub = lax.broadcasted_iota(jnp.int32, table.shape, 0)
    mask = (sub == lax.axis_index("expert")) & (owners_ref[...] == lax.axis_index("dp") // 4)
    hit = jnp.sum(jnp.where(mask, table, 0.0), axis=0, keepdims=True)
    owned_ref[...] = jnp.sum(hit, axis=1, keepdims=True)
    for copy in copies:
        copy.wait()


def body(gradients, owners):
    _, mats, rows, cols = gradients.shape
    n_groups = lax.axis_size("expert")
    total_rows = rows * lax.axis_size("dp")
    any_space = pl.BlockSpec(memory_space=pl.ANY)
    vmem = pl.BlockSpec(memory_space=pltpu.VMEM)
    full = pltpu.VMEM((cols, cols), BF16)
    dma = pltpu.SemaphoreType.DMA
    early = (PIECE, BLK)
    late = (BLK, BLK)
    moved, whole = pl.pallas_call(
        functools.partial(kernel, total_rows, n_groups),
        out_shape=(
            pltpu.VMEM((mats, rows, cols), BF16),
            jax.ShapeDtypeStruct((8, 128), F32),
        ),
        in_specs=[any_space],
        out_specs=(vmem, vmem),
        scratch_shapes=[
            pltpu.VMEM((mats * rows, cols), BF16),
            pltpu.VMEM((RING, *early), BF16),
            pltpu.VMEM((RING, *late), BF16),
            pltpu.VMEM((RING - 1, *early), BF16),
            pltpu.VMEM((RING - 1, *late), BF16),
            pltpu.VMEM((RING, *early), BF16),
            pltpu.VMEM((RING, *late), BF16),
            pltpu.VMEM((RING, 8, 128), F32),
            full,
            full,
            full,
            full,
            full,
            full,
            pltpu.VMEM((mats * rows, cols), BF16),
            pltpu.VMEM((2 * RING, 8, 128), F32),
            pltpu.VMEM((n_groups, 8, 128), F32),
            dma((2,)),
            dma((2, 2 * RING)),
            dma((2, 2 * RING)),
            dma((2, RING - 1)),
            dma((2, RING - 1)),
            dma((2, RING - 1)),
            dma((2, RING)),
            dma((RING - 1,)),
            dma((RING,)),
            dma((2 * RING,)),
            dma((2 * RING,)),
            dma((2 * RING - 1,)),
            dma((2 * RING,)),
            dma((n_groups - 1,)),
            dma((n_groups,)),
        ],
        compiler_params=pltpu.CompilerParams(
            collective_id=0, has_side_effects=True, vmem_limit_bytes=40 * 1024 * 1024
        ),
    )(pltpu.with_memory_space_constraint(gradients, pltpu.HBM))
    return pl.pallas_call(
        functools.partial(finish, n_groups),
        out_shape=(
            jax.ShapeDtypeStruct(gradients.shape, BF16),
            jax.ShapeDtypeStruct((n_groups, mats), F32),
            jax.ShapeDtypeStruct((1, 1), F32),
        ),
        in_specs=[vmem, vmem, vmem],
        out_specs=(any_space, vmem, vmem),
        scratch_shapes=[dma((mats,))],
        compiler_params=pltpu.CompilerParams(vmem_limit_bytes=4 * 1024 * 1024),
    )(moved, whole, owners)


def solution(mesh):
    placed = (P("expert", None, "dp", None), P("expert", None))
    return jax.shard_map(
        body,
        mesh=mesh,
        in_specs=placed,
        out_specs=(P("expert", None, "dp", None), P(), P("expert", "dp")),
        check_vma=False,
    )
```

profile of v0, /device:TPU:1, one launch (start us, length us, event | category | flops | bytes accessed | tf_op | source)
XLA Modules:
  0.0 64.1 jit_solution(13705523413722069798)
XLA Ops:
  0.6 0.0 copy-start
  0.6 61.4 %shard_map.49 = (bf16[8,112,1024]{2,1,0:T(8,128)(2,1)S(1)}, f32[8,128]{1,0:T(8,128)S(1)}) custom-call(bf16[1,8,112,1024]{3,2,1,0:T(8,128)(2,1)} %g_ref.1), custom_call_target="tpu_custom_call" | custom-call | tf_op jit(solution)/shard_map/pallas_call | solution.py:410
  62.1 0.0 copy-done
  62.1 1.9 %shard_map.50 = (bf16[1,8,112,1024]{3,2,1,0:T(8,128)(2,1)}, f32[8,8]{1,0:T(8,128)}, f32[1,1]{1,0:T(1,128)}) custom-call(bf16[8,112,1024]{2,1,0:T(8,128)(2,1)S(1)} %get-tuple-element.5.u_ref, f32[8,128]{1,0:T(8,128)S(1)} %get-tuple-element.6.whole_ref, s32[1,8]{1,0:T(1,128)S(1)} %copy-done), custom_call_target="tpu_custom_call" | custom-call | tf_op jit(solution)/shard_map/pallas_call | solution.py:456
Async XLA Ops:
  0.6 61.5 %copy-start = (s32[1,8]{1,0:T(1,128)S(1)}, s32[1,8]{1,0:T(1,128)}, u32[]{:S(2)}) copy-start(s32[1,8]{1,0:T(1,128)} %owners_ref.1) | copy-start | bytes 100
where the time goes:
time: 64.2 us; the launch traced here: 64.1 us
  Pallas kernels  63.3 us (99%)
  between operations  0.81 us (1%)
    pallas_call x1, Pallas kernels, body(): pl.pallas_call(functools.partial(kernel, total_rows, n_groups), out_shape...  61.4 us
    pallas_call x1, Pallas kernels, body(): pl.pallas_call(functools.partial(finish, n_groups), out_shape=(jax.ShapeD...  1.88 us

commit v1 on v0

--- a/solution.py
+++ b/solution.py
@@ -14,9 +14,12 @@
 
 RING = 4
 BLK = 256
-HALF = BLK // 2
-EARLY = 3 * BLK
-PIECE = BLK + HALF
+STAGES = (
+    ((0, 0), (1, 0), (1, 1)),
+    ((2, 0), (2, 1), (2, 2)),
+    ((3, 0), (3, 1), (3, 2), (3, 3)),
+)
+COLUMNS = ((0, 2 * BLK), (2 * BLK, BLK), (3 * BLK, BLK))
 
 F32 = jnp.float32
 BF16 = jnp.bfloat16
@@ -37,12 +40,9 @@
     u_ref,
     whole_ref,
     x_ref,
-    pa_ref,
-    pb_ref,
-    ra_ref,
-    rb_ref,
-    aa_ref,
-    ab_ref,
+    piece_refs,
+    got_refs,
+    all_refs,
     tr_ref,
     s_ref,
     e1_ref,
@@ -53,6 +53,7 @@
     y_ref,
     rms_ref,
     tab_ref,
+    go_sem,
     local_sem,
     in_send,
     in_recv,
@@ -100,26 +101,32 @@
         )
 
     barrier = pltpu.get_barrier_semaphore()
-    greeted = []
-    for offset in range(RING):
-        for core in (c, 1 - c):
-            if offset == 0 and core is c:
-                continue
-            greeted.append((along_p(offset, core), group))
+
+    def greet(sem, dp, to_group=group):
+        pl.semaphore_signal(
+            sem, inc=1, device_id=(dp, to_group), device_id_type=pl.DeviceIdType.MESH
+        )
+
     for offset in range(1, RING):
-        for core in (c, 1 - c):
-            greeted.append((along_q(offset, core), group))
-    for offset in range(1, n_groups):
-        greeted.append((d, lax.rem(group + offset, n_groups)))
-    for who in greeted:
-        pl.semaphore_signal(barrier, inc=1, device_id=who, device_id_type=pl.DeviceIdType.MESH)
+        greet(barrier, along_p(offset, 0))
+        greet(barrier, along_q(offset, 0))
+
     own = pltpu.make_async_copy(
         g_ref.at[0, mine], x_ref.at[pl.ds(pl.multiple_of(c * rows, 16), rows)], local_sem.at[0]
     )
     own.start()
-    pl.semaphore_wait(barrier, len(greeted))
-
-    parts = (pl.ds(0, EARLY), pl.ds(EARLY, cols - EARLY))
+
+    @pl.when(c == 0)
+    def _():
+        pl.semaphore_wait(barrier, 4 * (RING - 1) + 1)
+        greet(go_sem, d + 1)
+
+    @pl.when(c == 1)
+    def _():
+        greet(barrier, d - 1)
+        pl.semaphore_wait(go_sem, 1)
+
+    parts = [pl.ds(*part) for part in COLUMNS]
 
     def slot(offset, core, part):
         return x_ref.at[pl.ds(pl.multiple_of((2 * offset + core) * rows, 16), rows), part]
@@ -148,6 +155,11 @@
             copy.start()
             sent.append(copy)
 
+    @pl.when(c == 1)
+    def _():
+        for offset in range(1, n_groups):
+            greet(barrier, d, lax.rem(group + offset, n_groups))
+
     def arrive(number):
         part = parts[number]
         for offset, core in ((0, 1 - c), (1, 0), (1, 1), (3, 0), (3, 1), (2, 0), (2, 1)):
@@ -166,28 +178,27 @@
     def on_diag(value):
         return jnp.sum(jnp.where(diag, value, 0.0), axis=0, keepdims=True)
 
-    own.wait()
-    arrive(0)
-    value = dot_t(x_ref[:, pl.ds(0, BLK)], x_ref[:, pl.ds(0, BLK)])
-    total = on_diag(value)
-    pa_ref[0, pl.ds(0, BLK)] = value.astype(BF16)
-    value = dot_t(x_ref[:, pl.ds(BLK, BLK)], x_ref[:, pl.ds(0, 2 * BLK)])
-    total += on_diag(value[:, BLK:])
-    pa_ref[0, pl.ds(BLK, HALF)] = value[:HALF, :BLK].astype(BF16)
-    pa_ref[1, pl.ds(BLK, HALF)] = value[HALF:, :BLK].astype(BF16)
-    pa_ref[1, pl.ds(0, BLK)] = value[:, BLK:].astype(BF16)
-    value = dot_t(x_ref[:, pl.ds(2 * BLK, BLK)], x_ref[:, pl.ds(0, 3 * BLK)])
-    total += on_diag(value[:, 2 * BLK :])
-    pa_ref[2, pl.ds(BLK, HALF)] = value[:HALF, :BLK].astype(BF16)
-    pa_ref[3, pl.ds(BLK, HALF)] = value[HALF:, :BLK].astype(BF16)
-    pa_ref[3, pl.ds(0, BLK)] = value[:, BLK : 2 * BLK].astype(BF16)
-    pa_ref[2, pl.ds(0, BLK)] = value[:, 2 * BLK :].astype(BF16)
-
-    def scatter(number, piece_ref, got_ref):
+    def partial_gram(number):
+        total = jnp.zeros((1, BLK), F32)
+        for i in sorted({i for i, _ in STAGES[number]}):
+            value = dot_t(x_ref[:, pl.ds(i * BLK, BLK)], x_ref[:, pl.ds(0, (i + 1) * BLK)])
+            total += on_diag(value[:, i * BLK :])
+            for j in range(i + 1):
+                place = STAGES[number].index((i, j)) * BLK
+                piece_refs[number][pl.ds(place, BLK)] = value[:, j * BLK : (j + 1) * BLK].astype(
+                    BF16
+                )
+        return total
+
+    def quarter(number, k):
+        share = len(STAGES[number]) * BLK // RING
+        return pl.ds(pl.multiple_of(k * share, share), share)
+
+    def scatter(number):
         for offset in (2, 1, 3):
             copy = remote(
-                piece_ref.at[lax.rem(q + offset, RING)],
-                got_ref.at[RING - 1 - offset],
+                piece_refs[number].at[quarter(number, lax.rem(q + offset, RING))],
+                got_refs[number].at[RING - 1 - offset],
                 rs_send.at[number, offset - 1],
                 rs_recv.at[number, RING - 1 - offset],
                 along_q(offset, c),
@@ -195,19 +206,25 @@
             copy.start()
             sent.append(copy)
 
-    def add_up(number, piece_ref, got_ref, all_ref):
+    def add_up(number):
+        got_ref = got_refs[number]
+        here = quarter(number, q)
         for index in range(RING - 1):
             remote(
-                piece_ref.at[0], got_ref.at[index], rs_send.at[number, 0], rs_recv.at[number, index], d
+                got_ref.at[index],
+                got_ref.at[index],
+                rs_send.at[number, 0],
+                rs_recv.at[number, index],
+                d,
             ).wait_recv()
-        all_ref[q] = (
-            (piece_ref[q].astype(F32) + got_ref[0].astype(F32))
+        all_refs[number][here] = (
+            (piece_refs[number][here].astype(F32) + got_ref[0].astype(F32))
             + (got_ref[1].astype(F32) + got_ref[2].astype(F32))
         ).astype(BF16)
         for offset in (2, 1, 3):
             copy = remote(
-                all_ref.at[q],
-                all_ref.at[q],
+                all_refs[number].at[here],
+                all_refs[number].at[here],
                 ag_send.at[number, offset - 1],
                 ag_recv.at[number, q],
                 along_q(offset, c),
@@ -215,21 +232,18 @@
             copy.start()
             sent.append(copy)
 
-    def collect(number, all_ref):
+    def collect(number):
         for offset in (1, 3, 2):
             k = lax.rem(q + offset, RING)
-            remote(
-                all_ref.at[k], all_ref.at[k], ag_send.at[number, 0], ag_recv.at[number, k], d
-            ).wait_recv()
-
-    scatter(0, pa_ref, ra_ref)
-
-    arrive(1)
-    value = dot_t(x_ref[:, pl.ds(EARLY, BLK)], x_ref[...])
-    total += on_diag(value[:, EARLY:])
-    for k in range(RING):
-        pb_ref[k] = value[:, k * BLK : (k + 1) * BLK].astype(BF16)
-    scatter(1, pb_ref, rb_ref)
+            part = all_refs[number].at[quarter(number, k)]
+            remote(part, part, ag_send.at[number, 0], ag_recv.at[number, k], d).wait_recv()
+
+    own.wait()
+    total = jnp.zeros((1, BLK), F32)
+    for number in range(len(STAGES)):
+        arrive(number)
+        total += partial_gram(number)
+        scatter(number)
     tr_ref[q] = jnp.broadcast_to(jnp.sum(total, axis=1, keepdims=True), (8, 128))
     for offset in (2, 1, 3):
         copy = remote(
@@ -237,8 +251,8 @@
         )
         copy.start()
         sent.append(copy)
-    add_up(0, pa_ref, ra_ref, aa_ref)
-    add_up(1, pb_ref, rb_ref, ab_ref)
+    for number in range(len(STAGES)):
+        add_up(number)
 
     for offset in (1, 3, 2):
         k = lax.rem(q + offset, RING)
@@ -268,35 +282,16 @@
     def block(i):
         return pl.ds(i * BLK, BLK)
 
-    collect(0, aa_ref)
-    for k, (i, j) in enumerate(((0, 0), (1, 1), (2, 2), (2, 1))):
-        one = (aa_ref[k, pl.ds(0, BLK)].astype(F32) * square).astype(BF16)
-        s_ref[block(i), block(j)] = one
-        if i != j:
-            s_ref[block(j), block(i)] = one.T
-        high = pl.ds((1 + k // 2) * BLK + (k % 2) * HALF, HALF)
-        one = (aa_ref[k, pl.ds(BLK, HALF)].astype(F32) * square).astype(BF16)
-        s_ref[high, block(0)] = one
-        s_ref[block(0), high] = one.T
-    collect(1, ab_ref)
-    for k in range(RING):
-        one = (ab_ref[k].astype(F32) * square).astype(BF16)
-        s_ref[block(3), block(k)] = one
-        if k < 3:
-            s_ref[block(k), block(3)] = one.T
-
-    def product(out_ref, left, right, plus, by, times):
-        for i in range(RING):
-            wide = pl.ds(0, (i + 1) * BLK)
-            value = by * plus[block(i), wide].astype(F32) + times * dot(
-                left[block(i), :], right[:, wide]
-            )
-            value = value.astype(BF16)
-            out_ref[block(i), wide] = value
-            for j in range(i):
-                out_ref[block(j), block(i)] = value[:, j * BLK : (j + 1) * BLK].T
-
-    product(e1_ref, s_ref, s_ref, s_ref, COEF_B, COEF_C)
+    def unpack(number):
+        collect(number)
+        for place, (i, j) in enumerate(STAGES[number]):
+            one = (all_refs[number][block(place)].astype(F32) * square).astype(BF16)
+            s_ref[block(i), block(j)] = one
+            if i != j:
+                s_ref[block(j), block(i)] = one.T
+
+    unpack(0)
+    unpack(1)
 
     for offset in range(1, RING):
         other = c * RING + lax.rem(p + offset, RING)
@@ -309,17 +304,37 @@
     for index in range(2 * RING):
         line = jnp.where(lane == index, rms_ref[index], line)
     tab_ref[group] = line
-    for offset in range(1, n_groups):
-        copy = remote(
+    def tell(offset, core):
+        return remote(
             tab_ref.at[group],
             tab_ref.at[group],
-            tab_send.at[offset - 1],
+            tab_send.at[2 * offset - 2 + core],
             tab_recv.at[group],
-            d,
+            chip + core,
             lax.rem(group + offset, n_groups),
         )
-        copy.start()
-        sent.append(copy)
+
+    @pl.when(c == 1)
+    def _():
+        pl.semaphore_wait(barrier, n_groups - 1)
+        for offset in range(1, n_groups):
+            for core in (0, 1):
+                tell(offset, core).start()
+
+    unpack(2)
+
+    def product(out_ref, left, right, plus, by, times):
+        for i in range(RING):
+            wide = pl.ds(0, (i + 1) * BLK)
+            value = by * plus[block(i), wide].astype(F32) + times * dot(
+                left[block(i), :], right[:, wide]
+            )
+            value = value.astype(BF16)
+            out_ref[block(i), wide] = value
+            for j in range(i):
+                out_ref[block(j), block(i)] = value[:, j * BLK : (j + 1) * BLK].T
+
+    product(e1_ref, s_ref, s_ref, s_ref, COEF_B, COEF_C)
 
     product(r_ref, e1_ref, s_ref, s_ref, COEF_A, 1.0)
     product(a1_ref, e1_ref, r_ref, r_ref, COEF_A, 1.0)
@@ -378,6 +393,12 @@
         all_columns(mine, offset, core).wait_send()
     for copy in sent:
         copy.wait_send()
+
+    @pl.when(c == 1)
+    def _():
+        for offset in range(1, n_groups):
+            for core in (0, 1):
+                tell(offset, core).wait_send()
 
 
 def finish(n_groups, u_ref, whole_ref, owners_ref, update_ref, table_ref, owned_ref, sem):
@@ -405,8 +426,7 @@
     vmem = pl.BlockSpec(memory_space=pltpu.VMEM)
     full = pltpu.VMEM((cols, cols), BF16)
     dma = pltpu.SemaphoreType.DMA
-    early = (PIECE, BLK)
-    late = (BLK, BLK)
+    stacks = [len(stage) * BLK for stage in STAGES]
     moved, whole = pl.pallas_call(
         functools.partial(kernel, total_rows, n_groups),
         out_shape=(
@@ -417,12 +437,9 @@
         out_specs=(vmem, vmem),
         scratch_shapes=[
             pltpu.VMEM((mats * rows, cols), BF16),
-            pltpu.VMEM((RING, *early), BF16),
-            pltpu.VMEM((RING, *late), BF16),
-            pltpu.VMEM((RING - 1, *early), BF16),
-            pltpu.VMEM((RING - 1, *late), BF16),
-            pltpu.VMEM((RING, *early), BF16),
-            pltpu.VMEM((RING, *late), BF16),
+            tuple(pltpu.VMEM((stack, BLK), BF16) for stack in stacks),
+            tuple(pltpu.VMEM((RING - 1, stack // RING, BLK), BF16) for stack in stacks),
+            tuple(pltpu.VMEM((stack, BLK), BF16) for stack in stacks),
             pltpu.VMEM((RING, 8, 128), F32),
             full,
             full,
@@ -433,20 +450,21 @@
             pltpu.VMEM((mats * rows, cols), BF16),
             pltpu.VMEM((2 * RING, 8, 128), F32),
             pltpu.VMEM((n_groups, 8, 128), F32),
+            pltpu.SemaphoreType.REGULAR,
             dma((2,)),
-            dma((2, 2 * RING)),
-            dma((2, 2 * RING)),
-            dma((2, RING - 1)),
-            dma((2, RING - 1)),
-            dma((2, RING - 1)),
-            dma((2, RING)),
+            dma((len(STAGES), 2 * RING)),
+            dma((len(STAGES), 2 * RING)),
+            dma((len(STAGES), RING - 1)),
+            dma((len(STAGES), RING - 1)),
+            dma((len(STAGES), RING - 1)),
+            dma((len(STAGES), RING)),
             dma((RING - 1,)),
             dma((RING,)),
             dma((2 * RING,)),
             dma((2 * RING,)),
             dma((2 * RING - 1,)),
             dma((2 * RING,)),
-            dma((n_groups - 1,)),
+            dma((2 * (n_groups - 1),)),
             dma((n_groups,)),
         ],
         compiler_params=pltpu.CompilerParams(

time: 64.2 us -> 57.3 us (0.89)
  Pallas kernels: 63.3 us -> 56.4 us
    pallas_call x1, Pallas kernels: 61.4 us -> 54.5 us  [body(): pl.pallas_call(functools.partial(kernel, total_rows, n_groups), out_shape...]
where the time goes in v1:
time: 57.3 us; the launch traced here: 57.2 us
  Pallas kernels  56.4 us (98%)
  between operations  0.81 us (1%)
    pallas_call x1, Pallas kernels, body(): pl.pallas_call(functools.partial(kernel, total_rows, n_groups), out_shape...  54.5 us
    pallas_call x1, Pallas kernels, body(): pl.pallas_call(functools.partial(finish, n_groups), out_shape=(jax.ShapeD...  1.88 us

profile of v1, /device:TPU:1, one launch (start us, length us, event | category | flops | bytes accessed | tf_op | source)
XLA Modules:
  0.0 57.2 jit_solution(1032649572381620990)
XLA Ops:
  0.6 0.0 copy-start
  0.6 54.5 %shard_map.49 = (bf16[8,112,1024]{2,1,0:T(8,128)(2,1)S(1)}, f32[8,128]{1,0:T(8,128)S(1)}) custom-call(bf16[1,8,112,1024]{3,2,1,0:T(8,128)(2,1)} %g_ref.1), custom_call_target="tpu_custom_call" | custom-call | tf_op jit(solution)/shard_map/pallas_call | solution.py:430
  55.2 0.0 copy-done
  55.2 1.9 %shard_map.50 = (bf16[1,8,112,1024]{3,2,1,0:T(8,128)(2,1)}, f32[8,8]{1,0:T(8,128)}, f32[1,1]{1,0:T(1,128)}) custom-call(bf16[8,112,1024]{2,1,0:T(8,128)(2,1)S(1)} %get-tuple-element.5.u_ref, f32[8,128]{1,0:T(8,128)S(1)} %get-tuple-element.6.whole_ref, s32[1,8]{1,0:T(1,128)S(1)} %copy-done), custom_call_target="tpu_custom_call" | custom-call | tf_op jit(solution)/shard_map/pallas_call | solution.py:474
Async XLA Ops:
  0.6 54.5 %copy-start = (s32[1,8]{1,0:T(1,128)S(1)}, s32[1,8]{1,0:T(1,128)}, u32[]{:S(2)}) copy-start(s32[1,8]{1,0:T(1,128)} %owners_ref.1) | copy-start | bytes 100

commit v2 on v1

--- a/solution.py
+++ b/solution.py
@@ -14,12 +14,16 @@
 
 RING = 4
 BLK = 256
-STAGES = (
-    ((0, 0), (1, 0), (1, 1)),
-    ((2, 0), (2, 1), (2, 2)),
-    ((3, 0), (3, 1), (3, 2), (3, 3)),
-)
-COLUMNS = ((0, 2 * BLK), (2 * BLK, BLK), (3 * BLK, BLK))
+TILE = 128
+STAGES = (((0, BLK), (BLK, BLK)), ((2 * BLK, BLK),), ((3 * BLK, TILE),), ((3 * BLK + TILE, TILE),))
+FIRST_STAGES = len([stage for stage in STAGES if sum(stage[-1]) <= 3 * BLK])
+
+
+def tiles(stage):
+    first = stage[0][0] // TILE
+    last = sum(stage[-1]) // TILE
+    return [(i, j) for i in range(first, last) for j in range(i + 1)]
+
 
 F32 = jnp.float32
 BF16 = jnp.bfloat16
@@ -45,6 +49,7 @@
     all_refs,
     tr_ref,
     s_ref,
+    t_ref,
     e1_ref,
     r_ref,
     a1_ref,
@@ -126,7 +131,7 @@
         greet(barrier, d - 1)
         pl.semaphore_wait(go_sem, 1)
 
-    parts = [pl.ds(*part) for part in COLUMNS]
+    parts = [pl.ds(stage[0][0], sum(stage[-1]) - stage[0][0]) for stage in STAGES]
 
     def slot(offset, core, part):
         return x_ref.at[pl.ds(pl.multiple_of((2 * offset + core) * rows, 16), rows), part]
@@ -171,27 +176,26 @@
                 d,
             ).wait_recv()
 
-    diag = lax.broadcasted_iota(jnp.int32, (BLK, BLK), 0) == lax.broadcasted_iota(
-        jnp.int32, (BLK, BLK), 1
-    )
-
-    def on_diag(value):
-        return jnp.sum(jnp.where(diag, value, 0.0), axis=0, keepdims=True)
-
     def partial_gram(number):
-        total = jnp.zeros((1, BLK), F32)
-        for i in sorted({i for i, _ in STAGES[number]}):
-            value = dot_t(x_ref[:, pl.ds(i * BLK, BLK)], x_ref[:, pl.ds(0, (i + 1) * BLK)])
-            total += on_diag(value[:, i * BLK :])
-            for j in range(i + 1):
-                place = STAGES[number].index((i, j)) * BLK
-                piece_refs[number][pl.ds(place, BLK)] = value[:, j * BLK : (j + 1) * BLK].astype(
-                    BF16
-                )
+        total = jnp.zeros((1, 1), F32)
+        places = tiles(STAGES[number])
+        for first, count in STAGES[number]:
+            value = dot_t(x_ref[:, pl.ds(first, count)], x_ref[:, pl.ds(0, first + count)])
+            diag = lax.broadcasted_iota(jnp.int32, (count, count), 0) == lax.broadcasted_iota(
+                jnp.int32, (count, count), 1
+            )
+            line = jnp.sum(jnp.where(diag, value[:, first:], 0.0), axis=0, keepdims=True)
+            total += jnp.sum(line, axis=1, keepdims=True)
+            for down in range(0, count, TILE):
+                i = (first + down) // TILE
+                for j in range(i + 1):
+                    piece_refs[number][pl.ds(places.index((i, j)) * TILE, TILE)] = value[
+                        down : down + TILE, j * TILE : (j + 1) * TILE
+                    ].astype(BF16)
         return total
 
     def quarter(number, k):
-        share = len(STAGES[number]) * BLK // RING
+        share = len(tiles(STAGES[number])) * TILE // RING
         return pl.ds(pl.multiple_of(k * share, share), share)
 
     def scatter(number):
@@ -239,12 +243,12 @@
             remote(part, part, ag_send.at[number, 0], ag_recv.at[number, k], d).wait_recv()
 
     own.wait()
-    total = jnp.zeros((1, BLK), F32)
+    total = jnp.zeros((1, 1), F32)
     for number in range(len(STAGES)):
         arrive(number)
         total += partial_gram(number)
         scatter(number)
-    tr_ref[q] = jnp.broadcast_to(jnp.sum(total, axis=1, keepdims=True), (8, 128))
+    tr_ref[q] = jnp.broadcast_to(total, (8, 128))
     for offset in (2, 1, 3):
         copy = remote(
             tr_ref.at[q], tr_ref.at[q], tr_send.at[offset - 1], tr_recv.at[q], along_q(offset, c)
@@ -284,14 +288,16 @@
 
     def unpack(number):
         collect(number)
-        for place, (i, j) in enumerate(STAGES[number]):
-            one = (all_refs[number][block(place)].astype(F32) * square).astype(BF16)
-            s_ref[block(i), block(j)] = one
+        for place, (i, j) in enumerate(tiles(STAGES[number])):
+            down, right = pl.ds(i * TILE, TILE), pl.ds(j * TILE, TILE)
+            one = all_refs[number][pl.ds(place * TILE, TILE)].astype(F32) * square
+            one = one.astype(BF16)
+            s_ref[down, right] = one
             if i != j:
-                s_ref[block(j), block(i)] = one.T
-
-    unpack(0)
-    unpack(1)
+                s_ref[right, down] = one.T
+
+    for number in range(FIRST_STAGES):
+        unpack(number)
 
     for offset in range(1, RING):
         other = c * RING + lax.rem(p + offset, RING)
@@ -321,40 +327,75 @@
             for core in (0, 1):
                 tell(offset, core).start()
 
-    unpack(2)
-
-    def product(out_ref, left, right, plus, by, times):
-        for i in range(RING):
+    early = 3 * BLK
+    for i in range(RING - 1):
+        wide = pl.ds(0, (i + 1) * BLK)
+        t_ref[block(i), wide] = COEF_B * s_ref[block(i), wide].astype(F32) + COEF_C * dot(
+            s_ref[block(i), pl.ds(0, early)], s_ref[pl.ds(0, early), wide]
+        )
+    for number in range(FIRST_STAGES, len(STAGES)):
+        unpack(number)
+
+    def turn_over(out_ref, i, value):
+        value = value.astype(BF16)
+        out_ref[block(i), pl.ds(0, (i + 1) * BLK)] = value
+        for j in range(i):
+            out_ref[block(j), block(i)] = value[:, j * BLK : (j + 1) * BLK].T
+
+    def product(out_ref, left, right, plus, by, times, first=0):
+        for i in range(first, RING):
             wide = pl.ds(0, (i + 1) * BLK)
             value = by * plus[block(i), wide].astype(F32) + times * dot(
                 left[block(i), :], right[:, wide]
             )
-            value = value.astype(BF16)
-            out_ref[block(i), wide] = value
-            for j in range(i):
-                out_ref[block(j), block(i)] = value[:, j * BLK : (j + 1) * BLK].T
-
-    product(e1_ref, s_ref, s_ref, s_ref, COEF_B, COEF_C)
+            turn_over(out_ref, i, value)
+
+    for i in range(RING - 1):
+        wide = pl.ds(0, (i + 1) * BLK)
+        value = t_ref[block(i), wide] + COEF_C * dot(s_ref[block(i), block(3)], s_ref[block(3), wide])
+        turn_over(e1_ref, i, value)
+    product(e1_ref, s_ref, s_ref, s_ref, COEF_B, COEF_C, RING - 1)
 
     product(r_ref, e1_ref, s_ref, s_ref, COEF_A, 1.0)
     product(a1_ref, e1_ref, r_ref, r_ref, COEF_A, 1.0)
-    product(e2_ref, a1_ref, a1_ref, a1_ref, COEF_B, COEF_C)
+    def column(out_ref, left, right, plus, by, times, n):
+        down = pl.ds(n * BLK, cols - n * BLK)
+        value = by * plus(down, block(n)) + times * dot(left[down, :], right[:, block(n)])
+        value = value.astype(BF16)
+        out_ref[down, block(n)] = value
+        for i in range(n + 1, RING):
+            out_ref[block(n), block(i)] = value[(i - n) * BLK : (i - n + 1) * BLK, :].T
+
+    def second(n):
+        def plus(down, right):
+            return a1_ref[down, right].astype(F32)
+
+        column(e2_ref, a1_ref, a1_ref, plus, COEF_B, COEF_C, n)
+
 
     factor = math.sqrt(total_rows) * scale
     for n in range(RING):
-        both = e1_ref[:, block(n)].astype(F32) + e2_ref[:, block(n)].astype(F32)
-        e_ref[:, block(n)] = (COEF_A * both + dot(e1_ref[...], e2_ref[:, block(n)])).astype(BF16)
-        value = COEF_A * COEF_A * x_ref[:, block(n)].astype(F32) + dot(
-            x_ref[...], e_ref[:, block(n)]
-        )
-        y_ref[:, block(n)] = (factor * value).astype(BF16)
+        if n < 2:
+            for later in range(n, RING if n else 1):
+                second(later)
+
+        def plus(down, right):
+            return e1_ref[down, right].astype(F32) + e2_ref[down, right].astype(F32)
+
+        column(e_ref, e1_ref, e2_ref, plus, COEF_A, 1.0, n)
+
+        def update(span):
+            value = COEF_A * COEF_A * x_ref[span, block(n)].astype(F32) + dot(
+                x_ref[span, :], e_ref[:, block(n)]
+            )
+            y_ref[span, block(n)] = (factor * value).astype(BF16)
 
         def home(offset, core):
             return y_ref.at[
                 pl.ds(pl.multiple_of((2 * offset + core) * rows, 16), rows), block(n)
             ]
 
-        for offset, core in ((2, 0), (2, 1), (1, 0), (1, 1), (3, 0), (3, 1), (0, 1 - c)):
+        def back(offset, core):
             remote(
                 home(offset, core),
                 u_ref.at[mine, :, block(n)],
@@ -362,7 +403,18 @@
                 out_recv.at[mine],
                 along_p(offset, core),
             ).start()
-        pltpu.make_async_copy(home(0, c), u_ref.at[mine, :, block(n)], local_sem.at[1]).start()
+
+        if n:
+            update(pl.ds(0, 2 * RING * rows))
+        for offset in (2, 1, 3, 0):
+            if n == 0:
+                update(pl.ds(2 * offset * rows, 2 * rows))
+            if offset:
+                back(offset, 0)
+                back(offset, 1)
+            else:
+                back(0, 1 - c)
+                pltpu.make_async_copy(home(0, c), u_ref.at[mine, :, block(n)], local_sem.at[1]).start()
 
     for offset in range(1, n_groups):
         other = lax.rem(group + offset, n_groups)
@@ -426,7 +478,7 @@
     vmem = pl.BlockSpec(memory_space=pltpu.VMEM)
     full = pltpu.VMEM((cols, cols), BF16)
     dma = pltpu.SemaphoreType.DMA
-    stacks = [len(stage) * BLK for stage in STAGES]
+    stacks = [len(tiles(stage)) * TILE for stage in STAGES]
     moved, whole = pl.pallas_call(
         functools.partial(kernel, total_rows, n_groups),
         out_shape=(
@@ -437,11 +489,12 @@
         out_specs=(vmem, vmem),
         scratch_shapes=[
             pltpu.VMEM((mats * rows, cols), BF16),
-            tuple(pltpu.VMEM((stack, BLK), BF16) for stack in stacks),
-            tuple(pltpu.VMEM((RING - 1, stack // RING, BLK), BF16) for stack in stacks),
-            tuple(pltpu.VMEM((stack, BLK), BF16) for stack in stacks),
+            tuple(pltpu.VMEM((stack, TILE), BF16) for stack in stacks),
+            tuple(pltpu.VMEM((RING - 1, stack // RING, TILE), BF16) for stack in stacks),
+            tuple(pltpu.VMEM((stack, TILE), BF16) for stack in stacks),
             pltpu.VMEM((RING, 8, 128), F32),
             full,
+            pltpu.VMEM((3 * BLK, 3 * BLK), F32),
             full,
             full,
             full,

time: 57.3 us -> 55.4 us (0.967)
  Pallas kernels: 56.4 us -> 54.5 us
    pallas_call x1, Pallas kernels: 54.5 us -> 52.6 us  [body(): pl.pallas_call(functools.partial(kernel, total_rows, n_groups), out_shape...]
where the time goes in v2:
time: 55.4 us; the launch traced here: 55.3 us
  Pallas kernels  54.5 us (98%)
  between operations  0.81 us (1%)
    pallas_call x1, Pallas kernels, body(): pl.pallas_call(functools.partial(kernel, total_rows, n_groups), out_shape...  52.6 us
    pallas_call x1, Pallas kernels, body(): pl.pallas_call(functools.partial(finish, n_groups), out_shape=(jax.ShapeD...  1.88 us

profile of v2, /device:TPU:1, one launch (start us, length us, event | category | flops | bytes accessed | tf_op | source)
XLA Modules:
  0.0 55.3 jit_solution(14135175415909267160)
XLA Ops:
  0.6 0.0 copy-start
  0.6 52.6 %shard_map.49 = (bf16[8,112,1024]{2,1,0:T(8,128)(2,1)S(1)}, f32[8,128]{1,0:T(8,128)S(1)}) custom-call(bf16[1,8,112,1024]{3,2,1,0:T(8,128)(2,1)} %g_ref.1), custom_call_target="tpu_custom_call" | custom-call | tf_op jit(solution)/shard_map/pallas_call | solution.py:482
  53.3 0.0 copy-done
  53.3 1.9 %shard_map.50 = (bf16[1,8,112,1024]{3,2,1,0:T(8,128)(2,1)}, f32[8,8]{1,0:T(8,128)}, f32[1,1]{1,0:T(1,128)}) custom-call(bf16[8,112,1024]{2,1,0:T(8,128)(2,1)S(1)} %get-tuple-element.5.u_ref, f32[8,128]{1,0:T(8,128)S(1)} %get-tuple-element.6.whole_ref, s32[1,8]{1,0:T(1,128)S(1)} %copy-done), custom_call_target="tpu_custom_call" | custom-call | tf_op jit(solution)/shard_map/pallas_call | solution.py:527
Async XLA Ops:
  0.6 52.6 %copy-start = (s32[1,8]{1,0:T(1,128)S(1)}, s32[1,8]{1,0:T(1,128)}, u32[]{:S(2)}) copy-start(s32[1,8]{1,0:T(1,128)} %owners_ref.1) | copy-start | bytes 100

commit v3 on v2

--- a/solution.py
+++ b/solution.py
@@ -165,9 +165,12 @@
         for offset in range(1, n_groups):
             greet(barrier, d, lax.rem(group + offset, n_groups))
 
-    def arrive(number):
+    def arrive(number, offsets=(0, 1, 3, 2)):
         part = parts[number]
-        for offset, core in ((0, 1 - c), (1, 0), (1, 1), (3, 0), (3, 1), (2, 0), (2, 1)):
+        slots = [(offset, core) for offset in offsets for core in (0, 1) if offset]
+        if 0 in offsets:
+            slots.insert(0, (0, 1 - c))
+        for offset, core in slots:
             remote(
                 g_ref.at[0, 0, :, part],
                 slot(offset, core, part),
@@ -179,8 +182,17 @@
     def partial_gram(number):
         total = jnp.zeros((1, 1), F32)
         places = tiles(STAGES[number])
+        chunks = [((0, 1, 3, 2), 0, 2 * RING)]
+        if number == len(STAGES) - 1:
+            chunks = [((0, 1), 0, 4), ((3,), 6, 2), ((2,), 4, 2)]
         for first, count in STAGES[number]:
-            value = dot_t(x_ref[:, pl.ds(first, count)], x_ref[:, pl.ds(0, first + count)])
+            value = None
+            for offsets, start, size in chunks:
+                if number == len(STAGES) - 1 and first == STAGES[number][0][0]:
+                    arrive(number, offsets)
+                here = pl.ds(start * rows, size * rows)
+                term = dot_t(x_ref[here, pl.ds(first, count)], x_ref[here, pl.ds(0, first + count)])
+                value = term if value is None else value + term
             diag = lax.broadcasted_iota(jnp.int32, (count, count), 0) == lax.broadcasted_iota(
                 jnp.int32, (count, count), 1
             )
@@ -245,7 +257,8 @@
     own.wait()
     total = jnp.zeros((1, 1), F32)
     for number in range(len(STAGES)):
-        arrive(number)
+        if number < len(STAGES) - 1:
+            arrive(number)
         total += partial_gram(number)
         scatter(number)
     tr_ref[q] = jnp.broadcast_to(total, (8, 128))
@@ -404,17 +417,23 @@
                 along_p(offset, core),
             ).start()
 
-        if n:
-            update(pl.ds(0, 2 * RING * rows))
         for offset in (2, 1, 3, 0):
-            if n == 0:
-                update(pl.ds(2 * offset * rows, 2 * rows))
+            update(pl.ds(2 * offset * rows, 2 * rows))
             if offset:
                 back(offset, 0)
                 back(offset, 1)
             else:
                 back(0, 1 - c)
                 pltpu.make_async_copy(home(0, c), u_ref.at[mine, :, block(n)], local_sem.at[1]).start()
+
+    for copy in sent:
+        copy.wait_send()
+
+    @pl.when(c == 1)
+    def _():
+        for offset in range(1, n_groups):
+            for core in (0, 1):
+                tell(offset, core).wait_send()
 
     for offset in range(1, n_groups):
         other = lax.rem(group + offset, n_groups)
@@ -443,14 +462,6 @@
         all_columns((1 - c) * RING + index, 0, 0).wait_recv()
     for offset, core in ((2, 0), (2, 1), (1, 0), (1, 1), (3, 0), (3, 1), (0, 1 - c)):
         all_columns(mine, offset, core).wait_send()
-    for copy in sent:
-        copy.wait_send()
-
-    @pl.when(c == 1)
-    def _():
-        for offset in range(1, n_groups):
-            for core in (0, 1):
-                tell(offset, core).wait_send()
 
 
 def finish(n_groups, u_ref, whole_ref, owners_ref, update_ref, table_ref, owned_ref, sem):

time: 55.4 us -> 54.9 us (level)
  no operation moved by 1% of the time
where the time goes in v3:
time: 54.9 us
  Pallas kernels  54 us (98%)
  between operations  0.81 us (1%)
    pallas_call x1, Pallas kernels, body(): pl.pallas_call(functools.partial(kernel, total_rows, n_groups), out_shape...  52.2 us
    pallas_call x1, Pallas kernels, body(): pl.pallas_call(functools.partial(finish, n_groups), out_shape=(jax.ShapeD...  1.88 us

profile of v3, /device:TPU:1, one launch (start us, length us, event | category | flops | bytes accessed | tf_op | source)
XLA Modules:
  0.0 54.9 jit_solution(1033748046533196142)
XLA Ops:
  0.6 0.0 copy-start
  0.6 52.2 %shard_map.49 = (bf16[8,112,1024]{2,1,0:T(8,128)(2,1)S(1)}, f32[8,128]{1,0:T(8,128)S(1)}) custom-call(bf16[1,8,112,1024]{3,2,1,0:T(8,128)(2,1)} %g_ref.1), custom_call_target="tpu_custom_call" | custom-call | tf_op jit(solution)/shard_map/pallas_call | solution.py:493
  52.8 0.0 copy-done
  52.8 1.9 %shard_map.50 = (bf16[1,8,112,1024]{3,2,1,0:T(8,128)(2,1)}, f32[8,8]{1,0:T(8,128)}, f32[1,1]{1,0:T(1,128)}) custom-call(bf16[8,112,1024]{2,1,0:T(8,128)(2,1)S(1)} %get-tuple-element.5.u_ref, f32[8,128]{1,0:T(8,128)S(1)} %get-tuple-element.6.whole_ref, s32[1,8]{1,0:T(1,128)S(1)} %copy-done), custom_call_target="tpu_custom_call" | custom-call | tf_op jit(solution)/shard_map/pallas_call | solution.py:538
Async XLA Ops:
  0.6 52.2 %copy-start = (s32[1,8]{1,0:T(1,128)S(1)}, s32[1,8]{1,0:T(1,128)}, u32[]{:S(2)}) copy-start(s32[1,8]{1,0:T(1,128)} %owners_ref.1) | copy-start | bytes 100

commit v4 on v3

--- a/solution.py
+++ b/solution.py
@@ -74,6 +74,8 @@
     rms_recv,
     tab_send,
     tab_recv,
+    whole_send,
+    whole_recv,
 ):
     rows = g_ref.shape[2]
     cols = g_ref.shape[3]
@@ -112,23 +114,32 @@
             sem, inc=1, device_id=(dp, to_group), device_id_type=pl.DeviceIdType.MESH
         )
 
+    def greet_unless_one(dp):
+        @pl.when(dp != 1)
+        def _():
+            greet(barrier, dp)
+
     for offset in range(1, RING):
-        greet(barrier, along_p(offset, 0))
-        greet(barrier, along_q(offset, 0))
+        for along in (along_p, along_q):
+            greet(barrier, along(offset, 0))
+            greet_unless_one(along(offset, 1))
+    greet_unless_one(chip + 1 - c)
 
     own = pltpu.make_async_copy(
         g_ref.at[0, mine], x_ref.at[pl.ds(pl.multiple_of(c * rows, 16), rows)], local_sem.at[0]
     )
     own.start()
 
-    @pl.when(c == 0)
+    @pl.when(d != 1)
     def _():
         pl.semaphore_wait(barrier, 4 * (RING - 1) + 1)
-        greet(go_sem, d + 1)
-
-    @pl.when(c == 1)
-    def _():
-        greet(barrier, d - 1)
+
+    @pl.when(d == 0)
+    def _():
+        greet(go_sem, 1)
+
+    @pl.when(d == 1)
+    def _():
         pl.semaphore_wait(go_sem, 1)
 
     parts = [pl.ds(stage[0][0], sum(stage[-1]) - stage[0][0]) for stage in STAGES]
@@ -160,7 +171,7 @@
             copy.start()
             sent.append(copy)
 
-    @pl.when(c == 1)
+    @pl.when(d == 1)
     def _():
         for offset in range(1, n_groups):
             greet(barrier, d, lax.rem(group + offset, n_groups))
@@ -323,22 +334,52 @@
     for index in range(2 * RING):
         line = jnp.where(lane == index, rms_ref[index], line)
     tab_ref[group] = line
-    def tell(offset, core):
+
+    def tell(offset):
         return remote(
             tab_ref.at[group],
             tab_ref.at[group],
-            tab_send.at[2 * offset - 2 + core],
+            tab_send.at[offset - 1],
             tab_recv.at[group],
-            chip + core,
+            d,
             lax.rem(group + offset, n_groups),
         )
 
-    @pl.when(c == 1)
+    @pl.when(d == 1)
     def _():
         pl.semaphore_wait(barrier, n_groups - 1)
         for offset in range(1, n_groups):
-            for core in (0, 1):
-                tell(offset, core).start()
+            tell(offset).start()
+
+    def along_row():
+        targets = [along_q(offset, core) for offset in range(1, RING) for core in (0, 1)]
+        return [
+            remote(whole_ref, whole_ref, whole_send.at[number], whole_recv, dp)
+            for number, dp in enumerate([d - 1, *targets])
+        ]
+
+    def along_column():
+        return [
+            remote(whole_ref, whole_ref, whole_send.at[2 * RING + up], whole_recv, d + 2 * RING * up)
+            for up in range(1, RING)
+        ]
+
+    def have_table():
+        remote(whole_ref, whole_ref, whole_send.at[0], whole_recv, d).wait_recv()
+
+    def share_table():
+        for offset in range(1, n_groups):
+            other = lax.rem(group + offset, n_groups)
+            remote(
+                tab_ref.at[other], tab_ref.at[other], tab_send.at[0], tab_recv.at[other], d
+            ).wait_recv()
+        sub = lax.broadcasted_iota(jnp.int32, (8, 128), 0)
+        whole = jnp.zeros((8, 128), F32)
+        for index in range(n_groups):
+            whole = jnp.where(sub == index, tab_ref[index], whole)
+        whole_ref[...] = whole
+        for copy in along_row():
+            copy.start()
 
     early = 3 * BLK
     for i in range(RING - 1):
@@ -425,26 +466,36 @@
             else:
                 back(0, 1 - c)
                 pltpu.make_async_copy(home(0, c), u_ref.at[mine, :, block(n)], local_sem.at[1]).start()
+        if n == 1:
+            pl.when(d == 1)(share_table)
 
     for copy in sent:
         copy.wait_send()
 
-    @pl.when(c == 1)
-    def _():
+    @pl.when((y == 0) & (d != 1))
+    def _():
+        have_table()
+
+    @pl.when(y == 0)
+    def _():
+        for copy in along_column():
+            copy.start()
+
+    @pl.when(y != 0)
+    def _():
+        have_table()
+
+    @pl.when(y == 0)
+    def _():
+        for copy in along_column():
+            copy.wait_send()
+
+    @pl.when(d == 1)
+    def _():
+        for copy in along_row():
+            copy.wait_send()
         for offset in range(1, n_groups):
-            for core in (0, 1):
-                tell(offset, core).wait_send()
-
-    for offset in range(1, n_groups):
-        other = lax.rem(group + offset, n_groups)
-        remote(
-            tab_ref.at[other], tab_ref.at[other], tab_send.at[0], tab_recv.at[other], d
-        ).wait_recv()
-    sub = lax.broadcasted_iota(jnp.int32, (8, 128), 0)
-    whole = jnp.zeros((8, 128), F32)
-    for index in range(n_groups):
-        whole = jnp.where(sub == index, tab_ref[index], whole)
-    whole_ref[...] = whole
+            tell(offset).wait_send()
 
     def all_columns(other, offset, core):
         return remote(
@@ -528,8 +579,10 @@
             dma((2 * RING,)),
             dma((2 * RING - 1,)),
             dma((2 * RING,)),
-            dma((2 * (n_groups - 1),)),
+            dma((n_groups - 1,)),
             dma((n_groups,)),
+            dma((3 * RING,)),
+            dma(()),
         ],
         compiler_params=pltpu.CompilerParams(
             collective_id=0, has_side_effects=True, vmem_limit_bytes=40 * 1024 * 1024

time: 54.9 us -> 54.7 us (level)
  no operation moved by 1% of the time
where the time goes in v4:
time: 54.7 us; the launch traced here: 54.6 us
  Pallas kernels  53.8 us (98%)
  between operations  0.81 us (1%)
    pallas_call x1, Pallas kernels, body(): pl.pallas_call(functools.partial(kernel, total_rows, n_groups), out_shape...  51.9 us
    pallas_call x1, Pallas kernels, body(): pl.pallas_call(functools.partial(finish, n_groups), out_shape=(jax.ShapeD...  1.88 us

profile of v4, /device:TPU:1, one launch (start us, length us, event | category | flops | bytes accessed | tf_op | source)
XLA Modules:
  0.0 54.6 jit_solution(4084721645825682000)
XLA Ops:
  0.6 0.0 copy-start
  0.6 51.9 %shard_map.49 = (bf16[8,112,1024]{2,1,0:T(8,128)(2,1)S(1)}, f32[8,128]{1,0:T(8,128)S(1)}) custom-call(bf16[1,8,112,1024]{3,2,1,0:T(8,128)(2,1)} %g_ref.1), custom_call_target="tpu_custom_call" | custom-call | tf_op jit(solution)/shard_map/pallas_call | solution.py:544
  52.5 0.0 copy-done
  52.5 1.9 %shard_map.50 = (bf16[1,8,112,1024]{3,2,1,0:T(8,128)(2,1)}, f32[8,8]{1,0:T(8,128)}, f32[1,1]{1,0:T(1,128)}) custom-call(bf16[8,112,1024]{2,1,0:T(8,128)(2,1)S(1)} %get-tuple-element.5.u_ref, f32[8,128]{1,0:T(8,128)S(1)} %get-tuple-element.6.whole_ref, s32[1,8]{1,0:T(1,128)S(1)} %copy-done), custom_call_target="tpu_custom_call" | custom-call | tf_op jit(solution)/shard_map/pallas_call | solution.py:591
Async XLA Ops:
  0.6 51.9 %copy-start = (s32[1,8]{1,0:T(1,128)S(1)}, s32[1,8]{1,0:T(1,128)}, u32[]{:S(2)}) copy-start(s32[1,8]{1,0:T(1,128)} %owners_ref.1) | copy-start | bytes 100
